TPU v7x, 512 devices: a whole 4x8x8 slice. The times are simulated.
512 devices in a mesh: seq: 64 (over y_lo, z, x), tp: 8 (over y_hi, core).
Axes of the slice: x: 4, y: 8 (y_hi: 4, y_lo: 2; y = y_hi * 2 + y_lo), z: 8, core: 2. Of those that a mesh axis runs over, the one named last changes fastest.
Arguments:
- query_act: bfloat16 [16384, 3072], P('seq', 'tp'), may hold values from -1200 to 1200
- key_act: bfloat16 [16384, 3072], P('seq', 'tp'), may hold values from -1200 to 1200
- value_act: bfloat16 [16384, 3072], P('seq', 'tp'), may hold values from -26 to 26
- hidden_act: bfloat16 [16384, 10240], P('seq', 'tp'), may hold values from -19 to 19
- conv_weight: float32 [27, 10240], P(None, 'tp'), may hold values from -1.25 to 1.25
- attention_grad: bfloat16 [16384, 3072], P('seq', 'tp'), may hold values from -26 to 26
- feedforward_grad: bfloat16 [16384, 10240], P('seq', 'tp'), may hold values from -6 to 6
Outputs:
- attention_out: bfloat16 [16384, 3072], P('seq', 'tp')
- feedforward_out: bfloat16 [16384, 10240], P('seq', 'tp')
- grad_query: bfloat16 [16384, 3072], P('seq', 'tp')
- grad_key: bfloat16 [16384, 3072], P('seq', 'tp')
- grad_value: bfloat16 [16384, 3072], P('seq', 'tp')
- grad_hidden: bfloat16 [16384, 10240], P('seq', 'tp')
All inputs are finite; a program needn't handle non-finite values.
Results may differ from a plain program's by a relative error of at most 0.0049.
Values may be sent and summed in bfloat16 or wider, within the bound.
A program may use at most 64 MiB of HBM per device.

v0:
```python
import jax
import jax.numpy as jnp
from jax import lax
from jax.sharding import PartitionSpec as P

HEADS = 24
HD = 128
HGT = 8
WID = 16


EPS = 1e-06
PRECISE = lax.Precision.HIGHEST


def padded_2(shard, sides, width):
    for axis, dim in sides:
        size, length = (lax.axis_size(axis), shard.shape[dim])
        up = [(i, (i + 1) % size) for i in range(size - 1)]
        down = [(j, i) for i, j in up]
        last = lax.slice_in_dim(shard, length - width, length, axis=dim)
        first = lax.slice_in_dim(shard, 0, width, axis=dim)
        before = lax.ppermute(last, axis, up)
        after = lax.ppermute(first, axis, down)
        shard = jnp.concatenate([before, shard, after], axis=dim)
    return shard


def unit_features(raw_values, totals, feature_count):
    row_scale = jnp.sqrt(totals / feature_count + EPS)
    return (jnp.maximum(raw_values, 0.0) / row_scale[:, None], row_scale)


def norm_backward(raw_values, row_scale, grad_feat, inner_total, feature_count):
    direct = jnp.where(raw_values > 0, grad_feat, 0.0) / row_scale[:, None]
    result = direct - (inner_total / (feature_count * row_scale * row_scale))[:, None] * raw_values
    return result.astype(jnp.bfloat16)


def padded_frames(source):
    rims = padded_2(source, (("seq", 0),), 1)
    return jnp.pad(rims, ((0, 0), (1, 1), (1, 1), (0, 0)))


def tap_sum(padded, weight, mirror):
    frames = padded.shape[0] - 2
    height = padded.shape[1] - 2
    breadth = padded.shape[2] - 2
    running = jnp.zeros((frames, height, breadth, padded.shape[3]), jnp.float32)
    for frame_off in range(3):
        for row_off in range(3):
            for col_off in range(3):
                tap_index = frame_off * 9 + row_off * 3 + col_off
                if mirror:
                    first_f, first_r, first_c = (2 - frame_off, 2 - row_off, 2 - col_off)
                else:
                    first_f, first_r, first_c = (frame_off, row_off, col_off)
                window = padded[
                    first_f : first_f + frames,
                    first_r : first_r + height,
                    first_c : first_c + breadth,
                ]
                running = running + weight[tap_index] * window.astype(jnp.float32)
    return running


def body(query_act, key_act, value_act, hidden_act, conv_weight, attention_grad, feedforward_grad):
    tokens_dev, local_cols = query_act.shape
    local_heads = local_cols // HD
    seq_tokens = tokens_dev * lax.axis_size("seq")
    feature_count = HEADS * HD
    query_vals = query_act.astype(jnp.float32)
    key_vals = key_act.astype(jnp.float32)
    query_sq, key_sq = lax.psum(
        (jnp.sum(query_vals * query_vals, axis=1), jnp.sum(key_vals * key_vals, axis=1)), "tp"
    )
    feat_query, scale_query = unit_features(query_vals, query_sq, feature_count)
    feat_key, scale_key = unit_features(key_vals, key_sq, feature_count)
    query3 = feat_query.reshape(tokens_dev, local_heads, HD)
    keys3 = feat_key.reshape(tokens_dev, local_heads, HD)
    value3 = value_act.astype(jnp.float32).reshape(tokens_dev, local_heads, HD)
    kv_part = jnp.einsum("thi,thj->hij", keys3, value3, precision=PRECISE) / seq_tokens
    norm_part = jnp.sum(keys3, axis=0) / seq_tokens
    kv_total, norm_total = lax.psum((kv_part, norm_part), "seq")
    numerator = jnp.einsum("thi,hij->thj", query3, kv_total, precision=PRECISE)
    denominator = 1.0 + jnp.einsum("thi,hi->th", query3, norm_total, precision=PRECISE) / HD
    attention = numerator / denominator[:, :, None]
    attention_out = attention.reshape(tokens_dev, local_cols).astype(jnp.bfloat16)
    frames = tokens_dev // (HGT * WID)
    hidden4 = hidden_act.reshape(frames, HGT, WID, -1)
    pre_act = tap_sum(padded_frames(hidden4), conv_weight, False)
    sigmoid_pre = jax.nn.sigmoid(pre_act)
    feedforward_out = (pre_act * sigmoid_pre).astype(jnp.bfloat16).reshape(tokens_dev, -1)
    grad_ff = feedforward_grad.reshape(pre_act.shape).astype(jnp.float32)
    grad_pre = (grad_ff * sigmoid_pre * (1.0 + pre_act * (1.0 - sigmoid_pre))).astype(jnp.bfloat16)
    grad_in = tap_sum(padded_frames(grad_pre), conv_weight, True)
    grad_hidden = grad_in.astype(jnp.bfloat16).reshape(tokens_dev, -1)
    grad3 = attention_grad.astype(jnp.float32).reshape(tokens_dev, local_heads, HD)
    grad_numer = grad3 / denominator[:, :, None]
    grad_denom = -jnp.sum(grad3 * attention, axis=2) / denominator / HD
    grad_fq = (
        jnp.einsum("thj,hij->thi", grad_numer, kv_total, precision=PRECISE)
        + grad_denom[:, :, None] * norm_total[None]
    )
    grad_fq = grad_fq.reshape(tokens_dev, local_cols)
    kv_grad_part = jnp.einsum("thi,thj->hij", query3, grad_numer, precision=PRECISE) / seq_tokens
    norm_grad_part = jnp.einsum("th,thi->hi", grad_denom, query3, precision=PRECISE) / seq_tokens
    query_inner = jnp.sum(feat_query * grad_fq, axis=1)
    kv_grad, norm_grad = lax.psum((kv_grad_part, norm_grad_part), "seq")
    grad_fk = jnp.einsum("thj,hij->thi", value3, kv_grad, precision=PRECISE) + norm_grad[None]
    grad_fk = grad_fk.reshape(tokens_dev, local_cols)
    grad_value = jnp.einsum("thi,hij->thj", keys3, kv_grad, precision=PRECISE)
    grad_value = grad_value.reshape(tokens_dev, local_cols).astype(jnp.bfloat16)
    key_inner = jnp.sum(feat_key * grad_fk, axis=1)
    query_total, key_total = lax.psum((query_inner, key_inner), "tp")
    grad_query = norm_backward(query_vals, scale_query, grad_fq, query_total, feature_count)
    grad_key = norm_backward(key_vals, scale_key, grad_fk, key_total, feature_count)
    return (attention_out, feedforward_out, grad_query, grad_key, grad_value, grad_hidden)


def solution(mesh):
    in_specs = (
        P("seq", "tp"),
        P("seq", "tp"),
        P("seq", "tp"),
        P("seq", "tp"),
        P(None, "tp"),
        P("seq", "tp"),
        P("seq", "tp"),
    )
    out_specs = (
        P("seq", "tp"),
        P("seq", "tp"),
        P("seq", "tp"),
        P("seq", "tp"),
        P("seq", "tp"),
        P("seq", "tp"),
    )
    return jax.shard_map(body, mesh=mesh, in_specs=in_specs, out_specs=out_specs, check_vma=False)
```

profile of v0, /device:TPU:1, one launch (start us, length us, event | category | flops | bytes accessed | tf_op | source)
XLA Modules:
  0.0 969.8 jit_solution(3188466887225778009)
XLA Ops:
  7.2 0.0 copy-start.6
  7.2 0.0 copy-start.7
  7.2 0.0 all-reduce.7.cloned.1.call-start
  7.2 2.0 fusion.31
  9.3 4.0 collective-permute-start
  13.2 0.0 copy-start.10
  13.2 1.4 collective-permute-start.1
  14.7 0.0 copy-done.6
  14.7 0.1 copy.33
  14.8 0.1 fusion.13
  14.9 0.1 copy.30
  15.1 0.1 fusion.9
  15.1 17.8 %all-reduce.4 = (f32[256]{0:T(256)S(1)}, f32[256]{0:T(256)S(1)}) all-reduce(f32[256]{0:T(256)S(1)} %fusion.9, f32[256]{0:T(256)S(1)} %fusion.13), channel_id=1, replica_groups=mesh['seq'=64,'tp'=8] {'tp'}, use_global_device_ids=true, to_apply=%region_1.0 | all-reduce | flops 512 | bytes 4096 | tf_op jit(solution)/shard_map/psum | solution.py:74
  33.0 0.5 copy-done.32
  33.5 0.2 fusion.29
  33.7 135.0 %psum.59 = f32[3,128]{1,0:T(4,128)S(1)} all-reduce(f32[3,128]{1,0:T(4,128)S(1)} %multiply_bitcast_fusion), channel_id=1, replica_groups=mesh['seq'=64,'tp'=8] {'seq'}, use_global_device_ids=true, to_apply=%region_6.0 | all-reduce | flops 384 | bytes 3072 | tf_op jit(solution)/shard_map/psum | solution.py:84
  168.7 0.3 fusion.25
  169.0 0.2 copy-done.36
  169.2 0.0 copy-done.10
  169.2 0.1 copy.36
  169.4 0.0 copy-start.4
  169.4 0.1 copy.31
  169.6 0.0 copy-start.11
  169.6 0.0 copy-start
  169.6 1.2 convolution_multiply_fusion
  170.8 1.0 convolution_multiply_fusion.1
  171.8 0.0 copy-done.4
  171.8 0.0 all-reduce.7.cloned.1.call-update
  171.8 0.0 copy-done.11
  171.9 0.1 slice_reduce_fusion.25
  172.0 0.0 copy-start.14
  172.0 0.0 copy-start.16
  172.1 0.3 slice_reduce_fusion.26
  172.3 0.0 collective-permute-done
  172.3 0.0 collective-permute-done.1
  172.4 0.0 copy-start.3
  172.4 0.9 select_maximum_fusion.2
  173.3 0.1 copy-done.3
  173.4 5.5 fusion.5
  178.9 0.9 fusion.30
  179.8 1.4 collective-permute-start.2
  181.3 1.3 collective-permute-start.3
  182.6 0.0 copy-start.31
  182.6 1.2 multiply_convert_fusion
  183.8 557.4 %all-reduce.7.cloned.1.call-done = (f32[3,128,128]{2,1,0:T(8,128)}, f32[3,128,128]{2,1,0:T(8,128)}) async-done(((f32[3,128,128]{2,1,0:T(8,128)}, f32[3,128,128]{2,1,0:T(8,128)}), (f32[3,128,128]{2,1,0:T(8,128)}, f32[3,128,128]{2,1,0:T(8,128)})) %all-reduce.7.cloned.1.call-update) | async-done | bytes 393232 | tf_op jit(solution)/shard_map/psum | solution.py:84
  741.2 2.2 multiply_reduce_fusion
  743.4 0.5 fusion.7
  744.0 0.1 fusion.19
  744.1 0.4 fusion.23
  744.5 128.4 %psum.62 = f32[3,128]{1,0:T(4,128)S(1)} all-reduce(f32[3,128]{1,0:T(4,128)S(1)} %bitcast_multiply_fusion.3), channel_id=1, replica_groups=mesh['seq'=64,'tp'=8] {'seq'}, use_global_device_ids=true, to_apply=%region_11.12 | all-reduce | flops 384 | bytes 3072 | tf_op jit(solution)/shard_map/psum | solution.py:109
  872.8 0.3 convolution_add_fusion
  873.2 0.1 fusion.17
  873.3 77.1 %all-reduce.3 = (f32[256]{0:T(256)S(1)}, f32[256]{0:T(256)S(1)}) all-reduce(f32[256]{0:T(256)S(1)} %fusion.19, f32[256]{0:T(256)S(1)} %fusion.17), channel_id=1, replica_groups=mesh['seq'=64,'tp'=8] {'tp'}, use_global_device_ids=true, to_apply=%region_9.10 | all-reduce | flops 512 | bytes 4096 | tf_op jit(solution)/shard_map/psum | solution.py:115
  950.4 0.1 fusion.11
  950.5 0.1 fusion.15
  950.6 0.8 copy.44
  951.4 0.8 copy.43
  952.2 0.8 copy.42
  953.1 0.5 convolution_convert_fusion
  953.6 0.8 copy.45
  954.5 0.0 collective-permute-done.2
  954.5 0.0 collective-permute-done.3
  954.5 1.9 select_maximum_fusion
  956.4 6.5 add_convert_fusion
  (81 shorter events, 0.2 us)
Async XLA Ops:
  7.2 7.5 copy-start.6
  7.2 7.7 copy-start.7
  7.2 734.0 %all-reduce.7.cloned.1.call-start = ((), (), s32[]{:S(2)}) async-start(), calls=%async_computation | async-start | bytes 786432 | tf_op jit(solution)/shard_map/psum | solution.py:84
  9.3 163.1 %collective-permute-start = (bf16[1,8,16,1280]{3,2,1,0:T(8,128)(2,1)}, bf16[1,8,16,1280]{3,2,1,0:T(8,128)(2,1)S(1)}, u32[]{:S(2)}, u32[]{:S(2)}) collective-permute-start(bf16[1,8,16,1280]{3,2,1,0:T(8,128)(2,1)} %bitcast.9), channel_id=1, source_target_pairs={{0,8},{8,16},{16,24},{24,32},{32,40},{40,48},{48,56},{56,64},{64,7... | collective-permute-start | bytes 983048 | tf_op jit(solution)/shard_map/ppermute | solution.py:23
  13.2 156.0 %copy-start.10 = (bf16[256,384]{1,0:T(8,128)(2,1)S(1)}, bf16[256,384]{1,0:T(8,128)(2,1)}, u32[]{:S(2)}) copy-start(bf16[256,384]{1,0:T(8,128)(2,1)} %param.12) | copy-start | bytes 589828
  13.2 159.1 %collective-permute-start.1 = (bf16[1,8,16,1280]{3,2,1,0:T(8,128)(2,1)}, bf16[1,8,16,1280]{3,2,1,0:T(8,128)(2,1)S(1)}, u32[]{:S(2)}, u32[]{:S(2)}) collective-permute-start(bf16[1,8,16,1280]{3,2,1,0:T(8,128)(2,1)} %bitcast.11), channel_id=1, source_target_pairs={{8,0},{16,8},{24,16},{32,24},{40,32},{48,40},{56,48},{64,56},{72,6... | collective-permute-start | bytes 983048 | tf_op jit(solution)/shard_map/ppermute | solution.py:24
  14.9 154.5 %copy-start.8 = (bf16[256,384]{1,0:T(8,128)(2,1)S(1)}, bf16[256,384]{1,0:T(8,128)(2,1)}, u32[]{:S(2)}) copy-start(bf16[256,384]{1,0:T(8,128)(2,1)} %param.9) | copy-start | bytes 589828
  32.9 136.0 %copy-start.40 = (f32[256]{0:T(256)}, f32[256]{0:T(256)S(1)}, u32[]{:S(2)}) copy-start(f32[256]{0:T(256)S(1)} %get-tuple-element.49) | copy-start | bytes 3076
  32.9 136.1 %copy-start.42 = (f32[256]{0:T(256)}, f32[256]{0:T(256)S(1)}, u32[]{:S(2)}) copy-start(f32[256]{0:T(256)S(1)} %get-tuple-element.50) | copy-start | bytes 3076
  32.9 0.6 copy-start.32
  33.5 135.2 %copy-start.34 = (f32[256]{0:T(256)}, f32[256]{0:T(256)S(1)}, u32[]{:S(2)}) copy-start(f32[256]{0:T(256)S(1)} %add_sqrt_fusion.1) | copy-start | bytes 3076
  168.7 0.6 copy-start.36
  169.2 2.6 copy-start.30
  169.2 2.6 copy-start.38
  169.4 2.4 copy-start.4
  169.6 2.3 copy-start.11
  169.6 2.8 copy-start
  172.0 1.3 copy-start.14
  172.0 1.3 copy-start.16
  172.0 1.3 copy-start.18
  172.0 1.3 copy-start.20
  172.0 1.3 copy-start.22
  172.0 1.3 copy-start.24
  172.0 1.3 copy-start.26
  172.0 1.3 copy-start.28
  172.3 1.0 copy-start.12
  172.4 1.1 copy-start.3
  179.8 561.3 %copy-start.5 = (f32[256,384]{0,1:T(8,128)S(1)}, f32[256,384]{0,1:T(8,128)}, u32[]{:S(2)}) copy-start(f32[256,384]{0,1:T(8,128)} %copy-done.4) | copy-start | bytes 1179652
  179.8 561.3 %copy-start.39 = (f32[256,3]{0,1:T(4,128)S(1)}, f32[256,3]{0,1:T(4,128)}, u32[]{:S(2)}) copy-start(f32[256,3]{0,1:T(4,128)} %copy-done.38) | copy-start | bytes 9220
  179.8 774.6 %collective-permute-start.2 = (bf16[1,8,16,1280]{3,2,1,0:T(8,128)(2,1)}, bf16[1,8,16,1280]{3,2,1,0:T(8,128)(2,1)S(1)}, u32[]{:S(2)}, u32[]{:S(2)}) collective-permute-start(bf16[1,8,16,1280]{3,2,1,0:T(8,128)(2,1)} %get-tuple-element.53), channel_id=1, source_target_pairs={{0,8},{8,16},{16,24},{24,32},{32,40},{40,48},{48,56},{56,64},{64,7... | collective-permute-start | bytes 983048 | tf_op jit(solution)/shard_map/ppermute | solution.py:23
  181.3 773.2 %collective-permute-start.3 = (bf16[1,8,16,1280]{3,2,1,0:T(8,128)(2,1)}, bf16[1,8,16,1280]{3,2,1,0:T(8,128)(2,1)}, u32[]{:S(2)}, u32[]{:S(2)}) collective-permute-start(bf16[1,8,16,1280]{3,2,1,0:T(8,128)(2,1)} %get-tuple-element.54), channel_id=1, source_target_pairs={{8,0},{16,8},{24,16},{32,24},{40,32},{48,40},{56,48},{64,56},{72,6... | collective-permute-start | bytes 983048 | tf_op jit(solution)/shard_map/ppermute | solution.py:24
  182.6 560.8 %copy-start.31 = (f32[3,1,256]{2,1,0:T(1,128)S(1)}, f32[3,1,256]{2,1,0:T(1,128)}, u32[]{:S(2)}) copy-start(f32[3,1,256]{2,1,0:T(1,128)} %copy-done.30) | copy-start | bytes 9220
  182.6 560.8 %copy-start.37 = (f32[3,128]{1,0:T(4,128)S(1)}, f32[3,128]{1,0:T(4,128)}, u32[]{:S(2)}) copy-start(f32[3,128]{1,0:T(4,128)} %copy-done.36) | copy-start | bytes 4612
  741.2 2.2 copy-start.44
  741.2 2.8 copy-start.33
  743.4 129.5 %copy-start.1 = (f32[3,128,128]{2,1,0:T(8,128)S(1)}, f32[3,128,128]{2,1,0:T(8,128)}, u32[]{:S(2)}) copy-start(f32[3,128,128]{2,1,0:T(8,128)} %get-tuple-element.46) | copy-start | bytes 589828
  743.4 129.7 %copy-start.35 = (f32[256]{0:T(256)S(1)}, f32[256]{0:T(256)}, u32[]{:S(2)}) copy-start(f32[256]{0:T(256)} %copy-done.34) | copy-start | bytes 3076
  743.9 206.5 %copy-start.41 = (f32[256]{0:T(256)S(1)}, f32[256]{0:T(256)}, u32[]{:S(2)}) copy-start(f32[256]{0:T(256)} %copy-done.40) | copy-start | bytes 3076
  743.9 206.4 %copy-start.43 = (f32[256]{0:T(256)S(1)}, f32[256]{0:T(256)}, u32[]{:S(2)}) copy-start(f32[256]{0:T(256)} %copy-done.42) | copy-start | bytes 3076
  873.3 79.0 %copy-start.9 = (bf16[256,3,128]{0,2,1:T(8,128)(2,1)S(1)}, bf16[256,3,128]{0,2,1:T(8,128)(2,1)}, u32[]{:S(2)}) copy-start(bf16[256,3,128]{0,2,1:T(8,128)(2,1)} %get-tuple-element.58) | copy-start | bytes 589828
  950.4 2.7 copy-start.2
  954.4 1.9 copy-start.13
  954.4 2.0 copy-start.15
  954.4 2.0 copy-start.17
  954.4 2.0 copy-start.19
  954.4 2.0 copy-start.21
  954.4 2.0 copy-start.23
  954.4 2.0 copy-start.25
  954.5 2.0 copy-start.27
  954.5 2.0 copy-start.29
Sparse Core Ops, SparseCore 0:
  172.0 569.1 all-reduce.6
where the time goes:
time: 972 us; the launch traced here: 970 us
  waiting for transfers between devices  557 us (57%)
  blocking collectives  358 us (37%)
  other arithmetic  16.7 us (2%)
  between operations  14.7 us (2%)
    psum x1, waiting for transfers between devices, body(): kv_total, norm_total = lax.psum((kv_part, norm_part), 'seq')  557 us
    psum x1, blocking collectives, body(): kv_total, norm_total = lax.psum((kv_part, norm_part), 'seq')  135 us
    psum x1, blocking collectives, body(): kv_grad, norm_grad = lax.psum((kv_grad_part, norm_grad_part), 'seq')  128 us
    psum x1, blocking collectives, body(): query_total, key_total = lax.psum((query_inner, key_inner), 'tp')  77.1 us
  transfers between devices with their start and end apart: 5, of which 1 were waited for; matrix products, arithmetic and copies ran while one was open for 2% of the time, Pallas kernels for 0%

commit v1 on v0

v1 whole, which is shorter than its diff:
```python
import functools

import jax
import jax.numpy as jnp
from jax import lax
from jax.experimental import pallas as pl
from jax.experimental.pallas import tpu as pltpu
from jax.sharding import PartitionSpec as P

HEADS = 24
HD = 128
HGT = 8
WID = 16
EPS = 1e-06

F32 = jnp.float32
BF16 = jnp.bfloat16

TOK = 256
FRAME = HGT * WID
HEADS_DEV = 3
COLS = HEADS_DEV * HD
CHAN = 1280
PAD_ROWS = FRAME + 2 * WID
FEATURES = HEADS * HD
TOKENS = 16384

NX, NZ, NYL = 4, 8, 2
NYH, NCORE = 4, 2
PLANE = NX * NYL
CHUNK = COLS // PLANE
HALO_COLS = 256
HALO_PARTS = CHAN // HALO_COLS
SEQ = NX * NZ * NYL
VMEM_LIMIT = 58 * 1024 * 1024


def nn(a, b):
    return lax.dot_general(a, b, (((1,), (0,)), ((), ())), preferred_element_type=F32)


def nt(a, b):
    return lax.dot_general(a, b, (((1,), (1,)), ((), ())), preferred_element_type=F32)


def tn(a, b):
    return lax.dot_general(a, b, (((0,), (0,)), ((), ())), preferred_element_type=F32)


def row_sums(x):
    ones = jnp.ones((8, x.shape[1]), BF16)
    high, low = split(x)
    return nt(ones, high) + nt(ones, low)


def as_columns(rows, first, count):
    lane = lax.broadcasted_iota(jnp.int32, (8, count * HD), 1) // HD
    row = lax.broadcasted_iota(jnp.int32, (8, count * HD), 0)
    pick = jnp.where(row == lane + first, 1.0, 0.0).astype(F32)
    return lax.dot_general(
        rows, pick, (((0,), (0,)), ((), ())), preferred_element_type=F32, precision=lax.Precision.HIGHEST
    )


def split(x):
    high = x.astype(BF16)
    return high, (x - high.astype(F32)).astype(BF16)


def head(i):
    return pl.ds(i * HD, HD)


def kernel(
    q_in, k_in, v_in, g_in, h_in, fg_in, w_in,
    att_out, ff_out, gq_out, gk_out, gv_out, gh_out,
    q, k, v, g, fg, w, hp, gp,
    att_o, ff_o, gq_o, gk_o, gv_o, gh_o,
    fq, fql, fk, gn, gnl, rinv, dinv, gden, gfk,
    tp1, tp2, tp3,
    kvp, kvs, kv1, kvc, kv2, kvb,
    gkp, gks, gk1, gkc, gk2, gkb,
    z1, z2, zt, gz1, gz2, gzt,
    in_sem, out_sem,
    tp_send, tp_recv, plane_send, plane_recv, ring_send, ring_recv,
    halo_send, halo_recv,
):
    s = lax.axis_index("seq")
    t = lax.axis_index("tp")
    yl, z, x = s // (NZ * NX), (s // NX) % NZ, s % NX
    yh, core = t // NCORE, t % NCORE

    def seq_at(yl_, z_, x_):
        return (yl_ * NZ + z_) * NX + x_

    def plane_at(j):
        return (yl + j // NX) % NYL, (x + j % NX) % NX

    def plane_dev(j):
        yl_, x_ = plane_at(j)
        return {"seq": seq_at(yl_, z, x_), "tp": t}

    def ring_dev(j):
        return {"seq": seq_at(yl, (z + j) % NZ, x), "tp": t}

    def tp_dev(j):
        return {"seq": s, "tp": ((yh + j // NCORE) % NYH) * NCORE + (core + j % NCORE) % NCORE}

    def remote(src, dst, send, recv, device):
        return pltpu.make_async_remote_copy(
            src_ref=src, dst_ref=dst, send_sem=send, recv_sem=recv,
            device_id=device, device_id_type=pl.DeviceIdType.MESH,
        )

    me = yl * NX + x
    mine = pl.ds(pl.multiple_of(me * CHUNK, 16), CHUNK)

    def plane_rows(j):
        yl_, x_ = plane_at(j)
        return pl.ds(pl.multiple_of((yl_ * NX + x_) * CHUNK, 16), CHUNK)

    def tp_round(i, buf):
        return [remote(buf.at[0], buf.at[j], tp_send.at[i, j], tp_recv.at[i, j], tp_dev(j)) for j in range(1, 8)]

    def ring_round(i, src, dst):
        return [remote(src, dst.at[j], ring_send.at[i, j], ring_recv.at[i, j], ring_dev(j)) for j in range(1, NZ)]

    def plane_round(i, src, dst):
        return [remote(src, dst.at[j], plane_send.at[i, j], plane_recv.at[i, j], plane_dev(j)) for j in range(1, PLANE)]

    def plane_scatter(i, src, dst):
        return [
            remote(src.at[plane_rows(j)], dst.at[j], plane_send.at[i, j], plane_recv.at[i, j], plane_dev(j))
            for j in range(1, PLANE)
        ]

    def plane_gather(i, buf):
        return [
            remote(buf.at[mine], buf.at[mine], plane_send.at[i, j], plane_recv.at[i, j], plane_dev(j))
            for j in range(1, PLANE)
        ]

    sent = []

    def start(copies):
        for copy in copies:
            copy.start()
        sent.extend(copies)

    def arrived(copies):
        for copy in copies:
            copy.wait_recv()

    def total(own, buf, count):
        for j in range(1, count):
            own = own + buf[j].astype(F32)
        return own

    up = {"seq": (s + 1) % SEQ, "tp": t}
    down = {"seq": (s + SEQ - 1) % SEQ, "tp": t}
    body_rows = pl.ds(WID, FRAME)

    def halo_copies(i, part, buf, src_up, src_down):
        cols = pl.ds(part * HALO_COLS, HALO_COLS)
        to_next = remote(
            src_up(cols), buf.at[0, body_rows, cols], halo_send.at[i, 0, part], halo_recv.at[i, 0, part], up
        )
        to_prev = remote(
            src_down(cols), buf.at[3, body_rows, cols], halo_send.at[i, 1, part], halo_recv.at[i, 1, part], down
        )
        return to_next, to_prev

    def hidden_halo(part):
        return halo_copies(
            0, part, hp, lambda c: h_in.at[pl.ds(FRAME, FRAME), c], lambda c: h_in.at[pl.ds(0, FRAME), c]
        )

    def grad_halo(part):
        return halo_copies(1, part, gp, lambda c: gp.at[2, body_rows, c], lambda c: gp.at[1, body_rows, c])

    def halo_start(copies):
        @pl.when(s < SEQ - 1)
        def _():
            copies[0].start()

        @pl.when(s > 0)
        def _():
            copies[1].start()

    def halo_arrived(copies):
        @pl.when(s > 0)
        def _():
            copies[0].wait_recv()

        @pl.when(s < SEQ - 1)
        def _():
            copies[1].wait_recv()

    def halo_sent(copies):
        @pl.when(s < SEQ - 1)
        def _():
            copies[0].wait_send()

        @pl.when(s > 0)
        def _():
            copies[1].wait_send()

    barrier = pltpu.get_barrier_semaphore()
    partners = [tp_dev(j) for j in range(1, 8)] + [plane_dev(j) for j in range(1, PLANE)]
    partners += [ring_dev(j) for j in range(1, NZ)] + [up, down]
    for device in partners:
        pl.semaphore_signal(barrier, inc=1, device_id=device, device_id_type=pl.DeviceIdType.MESH)

    loads = [
        pltpu.make_async_copy(src, dst, in_sem.at[i])
        for i, (src, dst) in enumerate(
            [
                (q_in, q), (k_in, k), (v_in, v), (g_in, g), (w_in, w),
                (h_in.at[pl.ds(0, FRAME)], hp.at[1, body_rows]),
                (h_in.at[pl.ds(FRAME, FRAME)], hp.at[2, body_rows]),
                (fg_in, fg),
            ]
        )
    ]
    for copy in loads:
        copy.start()
    stores = [
        pltpu.make_async_copy(src, dst, out_sem.at[i])
        for i, (src, dst) in enumerate(
            [(att_o, att_out), (ff_o, ff_out), (gq_o, gq_out), (gk_o, gk_out), (gv_o, gv_out), (gh_o, gh_out)]
        )
    ]

    blank = jnp.zeros((4, WID, CHAN), BF16)
    for buf in (hp, gp):
        buf[:, 0:WID, :] = blank
        buf[:, PAD_ROWS - WID : PAD_ROWS, :] = blank

    @pl.when(s == 0)
    def _():
        hp[0, WID : WID + FRAME, :] = jnp.zeros((FRAME, CHAN), BF16)
        gp[0, WID : WID + FRAME, :] = jnp.zeros((FRAME, CHAN), BF16)

    @pl.when(s == SEQ - 1)
    def _():
        hp[3, WID : WID + FRAME, :] = jnp.zeros((FRAME, CHAN), BF16)
        gp[3, WID : WID + FRAME, :] = jnp.zeros((FRAME, CHAN), BF16)

    row8 = lax.broadcasted_iota(jnp.int32, (8, TOK), 0)
    loads[0].wait()
    loads[1].wait()
    squares = []
    for ref in (q, k):
        vals = ref[...].astype(F32)
        squares.append(row_sums(vals * vals))
    tp1[0] = jnp.where(row8 == 0, squares[0], squares[1])

    pl.semaphore_wait(barrier, len(partners))
    round_sq = tp_round(0, tp1)
    start(round_sq)
    hidden = [hidden_halo(part) for part in range(HALO_PARTS)]
    grads = [grad_halo(part) for part in range(HALO_PARTS)]
    for copies in hidden:
        halo_start(copies)

    SPAN = 64
    cell = lax.broadcasted_iota(jnp.int32, (SPAN, HD), 0) % WID

    def tap_sum(buf, lanes, frame, row, mirror):
        sums = [None, None, None]
        for a in range(3):
            for b in range(3):
                block = buf[frame + a, pl.ds(row + b * WID, SPAN), lanes].astype(F32)
                for c in range(3):
                    tap = 9 * a + 3 * b + c
                    tap = 26 - tap if mirror else tap
                    term = w[pl.ds(tap, 1), lanes] * block
                    sums[c] = term if sums[c] is None else sums[c] + term
        left = jnp.where(cell == 0, 0.0, pltpu.roll(sums[0], 1, 0))
        right = jnp.where(cell == WID - 1, 0.0, pltpu.roll(sums[2], SPAN - 1, 0))
        return sums[1] + left + right

    TILES = HALO_COLS // HD
    SPANS = FRAME // SPAN

    def conv_step(part, store):
        def step(i, carry):
            lanes = pl.ds(pl.multiple_of(part * HALO_COLS + (i // (2 * SPANS)) * HD, HD), HD)
            store(lanes, (i // SPANS) % 2, pl.multiple_of((i % SPANS) * SPAN, SPAN))
            return carry

        lax.fori_loop(0, TILES * 2 * SPANS, step, 0)

    def forward(part):
        def store(lanes, frame, row):
            pre = tap_sum(hp, lanes, frame, row, False)
            sig = 1.0 / (1.0 + jnp.exp(-pre))
            at = pl.ds(pl.multiple_of(frame * FRAME + row, SPAN), SPAN)
            ff_o[at, lanes] = (pre * sig).astype(BF16)
            grad = fg[at, lanes].astype(F32) * sig * (1.0 + pre * (1.0 - sig))
            gp[frame + 1, pl.ds(pl.multiple_of(row + WID, WID), SPAN), lanes] = grad.astype(BF16)

        halo_arrived(hidden[part])
        conv_step(part, store)
        halo_start(grads[part])

    def backward(part):
        def store(lanes, frame, row):
            at = pl.ds(pl.multiple_of(frame * FRAME + row, SPAN), SPAN)
            gh_o[at, lanes] = tap_sum(gp, lanes, frame, row, True).astype(BF16)

        halo_arrived(grads[part])
        conv_step(part, store)

    for copy in loads[2:]:
        copy.wait()
    arrived(round_sq)
    squares = total(tp1[0], tp1, 8)
    rinv[...] = lax.rsqrt(as_columns(squares, 0, 2) * (1.0 / FEATURES) + EPS)

    z1[0] = jnp.zeros((8, HD), F32)
    gz1[0] = jnp.zeros((8, HD), F32)
    scale_k = rinv[:, HD : 2 * HD]
    for i in range(HEADS_DEV):
        feat = jnp.maximum(k[:, head(i)].astype(F32), 0.0) * scale_k
        z1[0, pl.ds(i, 1), :] = jnp.sum(feat, axis=0, keepdims=True) * (1.0 / TOKENS)
        feat = feat.astype(BF16)
        fk[:, head(i)] = feat
        kvp[head(i), :] = tn(feat, v[:, head(i)]) * (1.0 / TOKENS)
    kvs[...] = kvp[...].astype(BF16)
    round_kv1 = plane_scatter(0, kvs, kv1)
    round_z1 = plane_round(1, z1.at[0], z1)
    start(round_z1)
    start(round_kv1)

    scale_q = rinv[:, 0:HD]
    for i in range(HEADS_DEV):
        fq[:, head(i)], fql[:, head(i)] = split(jnp.maximum(q[:, head(i)].astype(F32), 0.0) * scale_q)
    forward(0)
    forward(1)

    arrived(round_z1)
    z2[0] = total(z1[0], z1, PLANE)
    round_z2 = ring_round(0, z2.at[0], z2)
    start(round_z2)
    arrived(round_kv1)
    kvc[...] = total(kvp[mine, :], kv1, PLANE)
    kv2[0] = kvc[...].astype(BF16)
    round_kv2 = ring_round(1, kv2.at[0], kv2)
    start(round_kv2)

    forward(2)
    forward(3)
    forward(4)

    arrived(round_kv2)
    kvb[mine, :] = total(kvc[...], kv2, NZ).astype(BF16)
    round_kv3 = plane_gather(2, kvb)
    start(round_kv3)

    stores[1].start()

    arrived(round_z2)
    zt[...] = total(z2[0], z2, NZ)
    for i in range(HEADS_DEV):
        feat = fq[:, head(i)]
        key_sum = jnp.broadcast_to(zt[pl.ds(i, 1), :], (HD, HD)).astype(BF16)
        inv = 1.0 / (1.0 + nt(feat, key_sum) * (1.0 / HD))
        dinv[:, head(i)] = inv
        grad, low = split(g[:, head(i)].astype(F32) * inv)
        gn[:, head(i)] = grad
        gnl[:, head(i)] = low
        gkp[head(i), :] = tn(feat, grad) * (1.0 / TOKENS)
    gks[...] = gkp[...].astype(BF16)
    round_gk1 = plane_scatter(3, gks, gk1)
    start(round_gk1)

    backward(0)

    arrived(round_kv3)
    inner = None
    for i in range(HEADS_DEV):
        feat = fq[:, head(i)]
        inv = dinv[:, head(i)]
        mat = kvb[head(i), :]
        att = (nn(feat, mat) + nn(fql[:, head(i)], mat)) * inv
        att_o[:, head(i)] = att.astype(BF16)
        prod = g[:, head(i)].astype(F32) * att * inv
        inner = prod if inner is None else inner + prod
        grad = jnp.sum(prod, axis=1, keepdims=True) * jnp.full((1, HD), -1.0 / HD, F32)
        gden[:, head(i)] = grad
        gz1[0, pl.ds(i, 1), :] = jnp.sum(grad * feat.astype(F32), axis=0, keepdims=True) * (1.0 / TOKENS)
    round_gz1 = plane_round(4, gz1.at[0], gz1)
    start(round_gz1)
    arrived(round_gk1)
    gkc[...] = total(gkp[mine, :], gk1, PLANE)
    gk2[0] = gkc[...].astype(BF16)
    round_gk2 = ring_round(2, gk2.at[0], gk2)
    start(round_gk2)
    tp2[0] = row_sums(inner)
    round_qi = tp_round(1, tp2)
    start(round_qi)
    stores[0].start()

    backward(1)

    arrived(round_gz1)
    gz2[0] = total(gz1[0], gz1, PLANE)
    round_gz2 = ring_round(3, gz2.at[0], gz2)
    start(round_gz2)

    backward(2)

    arrived(round_gk2)
    gkb[mine, :] = total(gkc[...], gk2, NZ).astype(BF16)
    round_gk3 = plane_gather(5, gkb)
    start(round_gk3)

    arrived(round_qi)
    scale_q = rinv[:, 0:HD]
    coef = as_columns(total(tp2[0], tp2, 8), 0, 1) * scale_q * scale_q * (1.0 / FEATURES)
    for i in range(HEADS_DEV):
        raw = q[:, head(i)].astype(F32)
        mat = kvb[head(i), :]
        grad = nt(gn[:, head(i)], mat) + nt(gnl[:, head(i)], mat) + gden[:, head(i)] * zt[pl.ds(i, 1), :]
        gq_o[:, head(i)] = (jnp.where(raw > 0, grad, 0.0) * scale_q - coef * raw).astype(BF16)

    stores[2].start()

    arrived(round_gz2)
    gzt[...] = total(gz2[0], gz2, NZ)
    arrived(round_gk3)
    inner = None
    for i in range(HEADS_DEV):
        feat = fk[:, head(i)]
        mat = gkb[head(i), :]
        grad = nt(v[:, head(i)], mat) + gzt[pl.ds(i, 1), :]
        gfk[:, head(i)] = grad
        prod = feat.astype(F32) * grad
        inner = prod if inner is None else inner + prod
    tp3[0] = row_sums(inner)
    round_ki = tp_round(2, tp3)
    start(round_ki)
    for i in range(HEADS_DEV):
        gv_o[:, head(i)] = nn(fk[:, head(i)], gkb[head(i), :]).astype(BF16)

    stores[4].start()

    backward(3)
    backward(4)
    stores[5].start()

    arrived(round_ki)
    scale_k = rinv[:, HD : 2 * HD]
    coef = as_columns(total(tp3[0], tp3, 8), 0, 1) * scale_k * scale_k * (1.0 / FEATURES)
    for i in range(HEADS_DEV):
        raw = k[:, head(i)].astype(F32)
        gk_o[:, head(i)] = (jnp.where(raw > 0, gfk[:, head(i)], 0.0) * scale_k - coef * raw).astype(BF16)
    stores[3].start()

    for copy in sent:
        copy.wait_send()
    for copies in hidden + grads:
        halo_sent(copies)
    for copy in stores:
        copy.wait()


def store_all(*refs):
    sem = refs[18]
    loads = [pltpu.make_async_copy(refs[i], refs[12 + i], sem.at[0, i]) for i in range(6)]
    stores = [pltpu.make_async_copy(refs[12 + i], refs[6 + i], sem.at[1, i]) for i in range(6)]
    for copy in loads:
        copy.start()
    for load, store in zip(loads, stores):
        load.wait()
        store.start()
    for copy in stores:
        copy.wait()


def body(query_act, key_act, value_act, hidden_act, conv_weight, attention_grad, feedforward_grad):
    att = jax.ShapeDtypeStruct((TOK, COLS), BF16)
    conv = jax.ShapeDtypeStruct((TOK, CHAN), BF16)

    def vmem(shape, dtype):
        return pltpu.VMEM(shape, dtype)

    def state():
        return [
            vmem((COLS, HD), F32),
            vmem((COLS, HD), BF16),
            vmem((PLANE, CHUNK, HD), BF16),
            vmem((CHUNK, HD), F32),
            vmem((NZ, CHUNK, HD), BF16),
            vmem((COLS, HD), BF16),
        ]

    narrow = lambda dtype: vmem((TOK, COLS), dtype)
    wide = lambda: vmem((TOK, CHAN), BF16)
    padded = lambda: vmem((4, PAD_ROWS, CHAN), BF16)
    dma = pltpu.SemaphoreType.DMA
    outs = pl.pallas_call(
        kernel,
        out_shape=(att, conv, att, att, att, conv),
        in_specs=[pl.BlockSpec(memory_space=pl.ANY)] * 7,
        out_specs=(pl.BlockSpec(memory_space=pl.ANY),) * 6,
        scratch_shapes=[
            narrow(BF16), narrow(BF16), narrow(BF16), narrow(BF16), wide(), vmem((27, CHAN), F32), padded(), padded(),
            narrow(BF16), wide(), narrow(BF16), narrow(BF16), narrow(BF16), wide(),
            *[narrow(BF16)] * 5, vmem((TOK, 2 * HD), F32), narrow(F32), narrow(F32), narrow(F32),
            vmem((8, 8, TOK), F32), vmem((8, 8, TOK), F32), vmem((8, 8, TOK), F32),
            *state(), *state(),
            vmem((PLANE, 8, HD), F32), vmem((NZ, 8, HD), F32), vmem((8, HD), F32),
            vmem((PLANE, 8, HD), F32), vmem((NZ, 8, HD), F32), vmem((8, HD), F32),
            dma((8,)), dma((6,)),
            dma((3, 8)), dma((3, 8)), dma((6, PLANE)), dma((6, PLANE)), dma((4, NZ)), dma((4, NZ)),
            dma((2, 2, HALO_PARTS)), dma((2, 2, HALO_PARTS)),
        ],
        compiler_params=pltpu.CompilerParams(
            collective_id=0, has_side_effects=True, vmem_limit_bytes=VMEM_LIMIT
        ),
        name="token_mixing",
    )(query_act, key_act, value_act, attention_grad, hidden_act, feedforward_grad, conv_weight)
    return pl.pallas_call(
        store_all,
        out_shape=(att, conv, att, att, att, conv),
        in_specs=[pl.BlockSpec(memory_space=pl.ANY)] * 6,
        out_specs=(pl.BlockSpec(memory_space=pl.ANY),) * 6,
        scratch_shapes=[narrow(BF16), wide(), narrow(BF16), narrow(BF16), narrow(BF16), wide(), dma((2, 6))],
        compiler_params=pltpu.CompilerParams(vmem_limit_bytes=VMEM_LIMIT),
        name="store_results",
    )(*outs)


def solution(mesh):
    in_specs = (
        P("seq", "tp"),
        P("seq", "tp"),
        P("seq", "tp"),
        P("seq", "tp"),
        P(None, "tp"),
        P("seq", "tp"),
        P("seq", "tp"),
    )
    out_specs = (P("seq", "tp"),) * 6
    return jax.shard_map(body, mesh=mesh, in_specs=in_specs, out_specs=out_specs, check_vma=False)
```

time: 972 us -> 65.8 us (0.07)
  waiting for transfers between devices: 557 us -> 0 us
  blocking collectives: 358 us -> 0 us
  Pallas kernels: 0 us -> 65 us
  other arithmetic: 16.7 us -> 0 us
  between operations: 14.7 us -> 0.64 us
    psum x1 -> x0, waiting for transfers between devices: 557 us -> none  [body(): kv_total, norm_total = lax.psum((kv_part, norm_part), 'seq')]
    psum x4 -> x0, blocking collectives: 358 us -> none  [the longest x1 135 us: body(): kv_total, norm_total = lax.psum((kv_part, norm_part), 'seq')]
    pallas_call x0 -> x2, Pallas kernels: none -> 65 us  [the longest x1 62.5 us: body(): pl.pallas_call(kernel, out_shape=(att, conv, att, att, att, conv), in_spe...]
    convert_element_type x5 -> x0, other arithmetic: 13.3 us -> none  [the longest x1 6.47 us: body(): grad_hidden = grad_in.astype(jnp.bfloat16).reshape(tokens_dev, -1)]
  transfers between devices with their start and end apart: 5 -> 0, of which waited for: 1 -> 0; matrix products, arithmetic and copies ran while one was open for 2% -> 0% of each run, Pallas kernels for 0% -> 0%
where the time goes in v1:
time: 65.8 us; the launch traced here: 65.7 us
  Pallas kernels  65 us (99%)
    pallas_call x1, Pallas kernels, body(): pl.pallas_call(kernel, out_shape=(att, conv, att, att, att, conv), in_spe...  62.5 us
    pallas_call x1, Pallas kernels, body(): pl.pallas_call(store_all, out_shape=(att, conv, att, att, att, conv), in_...  2.55 us

profile of v1, /device:TPU:1, one launch (start us, length us, event | category | flops | bytes accessed | tf_op | source)
XLA Modules:
  0.0 65.7 jit_solution(13410424595784547886)
XLA Ops:
  0.6 62.5 %token_mixing.1 = (bf16[256,384]{1,0:T(8,128)(2,1)}, bf16[256,1280]{1,0:T(8,128)(2,1)}, bf16[256,384]{1,0:T(8,128)(2,1)}, bf16[256,384]{1,0:T(8,128)(2,1)}, bf16...) custom-call(bf16[256,384]{1,0:T(8,128)(2,1)} %q_in.1, bf16[256,384]{1,0:T(8,128)(2,1)} %k_in.1, bf16[256,384]{1,0:T(8,128)(2,1)} %v_in.1, ...), custom_call_target="tpu_custom_call" | custom-call | tf_op jit(solution)/shard_map/token_mixing/pallas_call | solution.py:503
  63.1 2.5 %store_results.1 = (bf16[256,384]{1,0:T(8,128)(2,1)}, bf16[256,1280]{1,0:T(8,128)(2,1)}, bf16[256,384]{1,0:T(8,128)(2,1)}, bf16[256,384]{1,0:T(8,128)(2,1)}, bf1...) custom-call(bf16[256,384]{1,0:T(8,128)(2,1)} %get-tuple-element.12.refs_0_, ...), custom_call_target="tpu_custom_call" | custom-call | tf_op jit(solution)/shard_map/store_results/pallas_call | solution.py:525

commit v2 on v1

--- a/solution.py
+++ b/solution.py
@@ -57,9 +57,8 @@
     lane = lax.broadcasted_iota(jnp.int32, (8, count * HD), 1) // HD
     row = lax.broadcasted_iota(jnp.int32, (8, count * HD), 0)
     pick = jnp.where(row == lane + first, 1.0, 0.0).astype(F32)
-    return lax.dot_general(
-        rows, pick, (((0,), (0,)), ((), ())), preferred_element_type=F32, precision=lax.Precision.HIGHEST
-    )
+    high = rows.astype(BF16).astype(F32)
+    return tn(high, pick) + tn(rows - high, pick)
 
 
 def split(x):
@@ -76,7 +75,7 @@
     att_out, ff_out, gq_out, gk_out, gv_out, gh_out,
     q, k, v, g, fg, w, hp, gp,
     att_o, ff_o, gq_o, gk_o, gv_o, gh_o,
-    fq, fql, fk, gn, gnl, rinv, dinv, gden, gfk,
+    fq, fql, fk, gn, gnl, qt, kt, rinv, rrow, srow, dinv, gfk,
     tp1, tp2, tp3,
     kvp, kvs, kv1, kvc, kv2, kvb,
     gkp, gks, gk1, gkc, gk2, gkb,
@@ -120,25 +119,29 @@
         return pl.ds(pl.multiple_of((yl_ * NX + x_) * CHUNK, 16), CHUNK)
 
     def tp_round(i, buf):
-        return [remote(buf.at[0], buf.at[j], tp_send.at[i, j], tp_recv.at[i, j], tp_dev(j)) for j in range(1, 8)]
+        return [remote(buf.at[0], buf.at[j], tp_send.at[i, j], tp_recv.at[i, j], tp_dev(j)) for j in tp_order]
 
     def ring_round(i, src, dst):
-        return [remote(src, dst.at[j], ring_send.at[i, j], ring_recv.at[i, j], ring_dev(j)) for j in range(1, NZ)]
+        return [remote(src, dst.at[j], ring_send.at[i, j], ring_recv.at[i, j], ring_dev(j)) for j in ring_order]
 
     def plane_round(i, src, dst):
-        return [remote(src, dst.at[j], plane_send.at[i, j], plane_recv.at[i, j], plane_dev(j)) for j in range(1, PLANE)]
+        return [remote(src, dst.at[j], plane_send.at[i, j], plane_recv.at[i, j], plane_dev(j)) for j in plane_order]
 
     def plane_scatter(i, src, dst):
         return [
             remote(src.at[plane_rows(j)], dst.at[j], plane_send.at[i, j], plane_recv.at[i, j], plane_dev(j))
-            for j in range(1, PLANE)
+            for j in plane_order
         ]
 
     def plane_gather(i, buf):
         return [
             remote(buf.at[mine], buf.at[mine], plane_send.at[i, j], plane_recv.at[i, j], plane_dev(j))
-            for j in range(1, PLANE)
+            for j in plane_order
         ]
+
+    tp_order = (4, 5, 2, 3, 6, 7, 1)
+    ring_order = (4, 3, 5, 2, 6, 1, 7)
+    plane_order = (6, 2, 5, 7, 1, 3, 4)
 
     sent = []
 
@@ -204,12 +207,6 @@
         @pl.when(s > 0)
         def _():
             copies[1].wait_send()
-
-    barrier = pltpu.get_barrier_semaphore()
-    partners = [tp_dev(j) for j in range(1, 8)] + [plane_dev(j) for j in range(1, PLANE)]
-    partners += [ring_dev(j) for j in range(1, NZ)] + [up, down]
-    for device in partners:
-        pl.semaphore_signal(barrier, inc=1, device_id=device, device_id_type=pl.DeviceIdType.MESH)
 
     loads = [
         pltpu.make_async_copy(src, dst, in_sem.at[i])
@@ -222,7 +219,14 @@
             ]
         )
     ]
-    for copy in loads:
+    for copy in loads[:2]:
+        copy.start()
+    barrier = pltpu.get_barrier_semaphore()
+    partners = [tp_dev(j) for j in tp_order] + [plane_dev(j) for j in plane_order]
+    partners += [ring_dev(j) for j in ring_order] + [up, down]
+    for device in partners:
+        pl.semaphore_signal(barrier, inc=1, device_id=device, device_id_type=pl.DeviceIdType.MESH)
+    for copy in loads[2:]:
         copy.start()
     stores = [
         pltpu.make_async_copy(src, dst, out_sem.at[i])
@@ -231,37 +235,37 @@
         )
     ]
 
-    blank = jnp.zeros((4, WID, CHAN), BF16)
-    for buf in (hp, gp):
-        buf[:, 0:WID, :] = blank
-        buf[:, PAD_ROWS - WID : PAD_ROWS, :] = blank
-
-    @pl.when(s == 0)
-    def _():
-        hp[0, WID : WID + FRAME, :] = jnp.zeros((FRAME, CHAN), BF16)
-        gp[0, WID : WID + FRAME, :] = jnp.zeros((FRAME, CHAN), BF16)
-
-    @pl.when(s == SEQ - 1)
-    def _():
-        hp[3, WID : WID + FRAME, :] = jnp.zeros((FRAME, CHAN), BF16)
-        gp[3, WID : WID + FRAME, :] = jnp.zeros((FRAME, CHAN), BF16)
+    hidden = [hidden_halo(part) for part in range(HALO_PARTS)]
+    grads = [grad_halo(part) for part in range(HALO_PARTS)]
 
     row8 = lax.broadcasted_iota(jnp.int32, (8, TOK), 0)
     loads[0].wait()
     loads[1].wait()
     squares = []
     for ref in (q, k):
-        vals = ref[...].astype(F32)
-        squares.append(row_sums(vals * vals))
+        vals = [ref[:, head(i)].astype(F32) for i in range(HEADS_DEV)]
+        squares.append(row_sums(vals[0] * vals[0] + vals[1] * vals[1] + vals[2] * vals[2]))
     tp1[0] = jnp.where(row8 == 0, squares[0], squares[1])
-
     pl.semaphore_wait(barrier, len(partners))
     round_sq = tp_round(0, tp1)
     start(round_sq)
-    hidden = [hidden_halo(part) for part in range(HALO_PARTS)]
-    grads = [grad_halo(part) for part in range(HALO_PARTS)]
-    for copies in hidden:
-        halo_start(copies)
+    halo_start(hidden[0])
+    halo_start(hidden[1])
+
+    blank = jnp.zeros((4, WID, CHAN), BF16)
+    for buf in (hp, gp):
+        buf[:, 0:WID, :] = blank
+        buf[:, PAD_ROWS - WID : PAD_ROWS, :] = blank
+
+    @pl.when(s == 0)
+    def _():
+        hp[0, WID : WID + FRAME, :] = jnp.zeros((FRAME, CHAN), BF16)
+        gp[0, WID : WID + FRAME, :] = jnp.zeros((FRAME, CHAN), BF16)
+
+    @pl.when(s == SEQ - 1)
+    def _():
+        hp[3, WID : WID + FRAME, :] = jnp.zeros((FRAME, CHAN), BF16)
+        gp[3, WID : WID + FRAME, :] = jnp.zeros((FRAME, CHAN), BF16)
 
     SPAN = 64
     cell = lax.broadcasted_iota(jnp.int32, (SPAN, HD), 0) % WID
@@ -302,7 +306,6 @@
 
         halo_arrived(hidden[part])
         conv_step(part, store)
-        halo_start(grads[part])
 
     def backward(part):
         def store(lanes, frame, row):
@@ -312,33 +315,40 @@
         halo_arrived(grads[part])
         conv_step(part, store)
 
+    for i in range(HEADS_DEV):
+        kt[head(i), :] = jnp.maximum(k[:, head(i)], 0).T
+        qt[head(i), :] = jnp.maximum(q[:, head(i)], 0).T
+    z1[0] = jnp.zeros((8, HD), F32)
+    gz1[0] = jnp.zeros((8, HD), F32)
+    srow[...] = jnp.zeros((8, TOK), F32)
     for copy in loads[2:]:
         copy.wait()
+    ones = jnp.ones((8, TOK), BF16)
     arrived(round_sq)
-    squares = total(tp1[0], tp1, 8)
-    rinv[...] = lax.rsqrt(as_columns(squares, 0, 2) * (1.0 / FEATURES) + EPS)
-
-    z1[0] = jnp.zeros((8, HD), F32)
-    gz1[0] = jnp.zeros((8, HD), F32)
-    scale_k = rinv[:, HD : 2 * HD]
-    for i in range(HEADS_DEV):
-        feat = jnp.maximum(k[:, head(i)].astype(F32), 0.0) * scale_k
-        z1[0, pl.ds(i, 1), :] = jnp.sum(feat, axis=0, keepdims=True) * (1.0 / TOKENS)
-        feat = feat.astype(BF16)
-        fk[:, head(i)] = feat
-        kvp[head(i), :] = tn(feat, v[:, head(i)]) * (1.0 / TOKENS)
-    kvs[...] = kvp[...].astype(BF16)
-    round_kv1 = plane_scatter(0, kvs, kv1)
+    rrow[...] = lax.rsqrt(total(tp1[0], tp1, 8) * (1.0 / FEATURES) + EPS)
+    scale_k = rrow[1:2, :]
+    for i in range(HEADS_DEV):
+        feat, low = split(kt[head(i), :].astype(F32) * scale_k)
+        z1[0, pl.ds(i, 1), :] = (nt(ones, feat) + nt(ones, low))[0:1] * (1.0 / TOKENS)
+        part = nn(feat, v[:, head(i)]) * (1.0 / TOKENS)
+        kvp[head(i), :] = part
+        kvs[head(i), :] = part.astype(BF16)
     round_z1 = plane_round(1, z1.at[0], z1)
     start(round_z1)
+    round_kv1 = plane_scatter(0, kvs, kv1)
     start(round_kv1)
-
+    halo_start(hidden[2])
+
+    rinv[...] = as_columns(rrow[...], 0, 2)
     scale_q = rinv[:, 0:HD]
+    scale_k = rinv[:, HD : 2 * HD]
     for i in range(HEADS_DEV):
         fq[:, head(i)], fql[:, head(i)] = split(jnp.maximum(q[:, head(i)].astype(F32), 0.0) * scale_q)
+        fk[:, head(i)] = (jnp.maximum(k[:, head(i)].astype(F32), 0.0) * scale_k).astype(BF16)
+        qt[head(i), :] = (qt[head(i), :].astype(F32) * rrow[0:1, :]).astype(BF16)
+
     forward(0)
     forward(1)
-
     arrived(round_z1)
     z2[0] = total(z1[0], z1, PLANE)
     round_z2 = ring_round(0, z2.at[0], z2)
@@ -348,114 +358,121 @@
     kv2[0] = kvc[...].astype(BF16)
     round_kv2 = ring_round(1, kv2.at[0], kv2)
     start(round_kv2)
+    halo_start(hidden[3])
+
 
     forward(2)
-    forward(3)
-    forward(4)
+    arrived(round_z2)
+    zt[...] = total(z2[0], z2, NZ)
+    for i in range(HEADS_DEV):
+        key_sum = jnp.broadcast_to(zt[pl.ds(i, 1), :], (HD, HD)).astype(BF16)
+        inv = 1.0 / (1.0 + nt(fq[:, head(i)], key_sum) * (1.0 / HD))
+        dinv[:, head(i)] = inv
+        grad, low = split(g[:, head(i)].astype(F32) * inv)
+        gn[:, head(i)] = grad
+        gnl[:, head(i)] = low
+        part = nn(qt[head(i), :], grad) * (1.0 / TOKENS)
+        gkp[head(i), :] = part
+        gks[head(i), :] = part.astype(BF16)
+    round_gk1 = plane_scatter(3, gks, gk1)
+    start(round_gk1)
 
     arrived(round_kv2)
     kvb[mine, :] = total(kvc[...], kv2, NZ).astype(BF16)
     round_kv3 = plane_gather(2, kvb)
     start(round_kv3)
-
-    stores[1].start()
-
-    arrived(round_z2)
-    zt[...] = total(z2[0], z2, NZ)
-    for i in range(HEADS_DEV):
-        feat = fq[:, head(i)]
-        key_sum = jnp.broadcast_to(zt[pl.ds(i, 1), :], (HD, HD)).astype(BF16)
-        inv = 1.0 / (1.0 + nt(feat, key_sum) * (1.0 / HD))
-        dinv[:, head(i)] = inv
-        grad, low = split(g[:, head(i)].astype(F32) * inv)
-        gn[:, head(i)] = grad
-        gnl[:, head(i)] = low
-        gkp[head(i), :] = tn(feat, grad) * (1.0 / TOKENS)
-    gks[...] = gkp[...].astype(BF16)
-    round_gk1 = plane_scatter(3, gks, gk1)
-    start(round_gk1)
-
-    backward(0)
-
-    arrived(round_kv3)
-    inner = None
-    for i in range(HEADS_DEV):
-        feat = fq[:, head(i)]
-        inv = dinv[:, head(i)]
-        mat = kvb[head(i), :]
-        att = (nn(feat, mat) + nn(fql[:, head(i)], mat)) * inv
-        att_o[:, head(i)] = att.astype(BF16)
-        prod = g[:, head(i)].astype(F32) * att * inv
-        inner = prod if inner is None else inner + prod
-        grad = jnp.sum(prod, axis=1, keepdims=True) * jnp.full((1, HD), -1.0 / HD, F32)
-        gden[:, head(i)] = grad
-        gz1[0, pl.ds(i, 1), :] = jnp.sum(grad * feat.astype(F32), axis=0, keepdims=True) * (1.0 / TOKENS)
-    round_gz1 = plane_round(4, gz1.at[0], gz1)
-    start(round_gz1)
+    halo_start(hidden[4])
+    forward(3)
+
     arrived(round_gk1)
     gkc[...] = total(gkp[mine, :], gk1, PLANE)
     gk2[0] = gkc[...].astype(BF16)
     round_gk2 = ring_round(2, gk2.at[0], gk2)
     start(round_gk2)
-    tp2[0] = row_sums(inner)
+    halo_start(grads[0])
+    halo_start(grads[1])
+
+    arrived(round_kv3)
+    for i in range(HEADS_DEV):
+        mat = kvb[head(i), :]
+        inv = dinv[:, head(i)]
+        att = (nn(fq[:, head(i)], mat) + nn(fql[:, head(i)], mat)) * inv
+        att_o[:, head(i)] = att.astype(BF16)
+        inner = row_sums(g[:, head(i)].astype(F32) * inv * att)
+        srow[pl.ds(i, 1), :] = inner[0:1]
+        high, low = split(inner)
+        feat = fq[:, head(i)]
+        gz1[0, pl.ds(i, 1), :] = (nn(high, feat) + nn(low, feat))[0:1] * (-1.0 / HD / TOKENS)
+    round_gz1 = plane_round(4, gz1.at[0], gz1)
+    start(round_gz1)
+    tp2[0] = jnp.broadcast_to(srow[0:1, :] + srow[1:2, :] + srow[2:3, :], (8, TOK))
     round_qi = tp_round(1, tp2)
     start(round_qi)
     stores[0].start()
-
-    backward(1)
-
+    forward(4)
+    stores[1].start()
+
+
+    arrived(round_gk2)
+    gkb[mine, :] = total(gkc[...], gk2, NZ).astype(BF16)
+    round_gk3 = plane_gather(5, gkb)
+    start(round_gk3)
     arrived(round_gz1)
     gz2[0] = total(gz1[0], gz1, PLANE)
     round_gz2 = ring_round(3, gz2.at[0], gz2)
     start(round_gz2)
-
-    backward(2)
-
-    arrived(round_gk2)
-    gkb[mine, :] = total(gkc[...], gk2, NZ).astype(BF16)
-    round_gk3 = plane_gather(5, gkb)
-    start(round_gk3)
+    halo_start(grads[2])
+    halo_start(grads[3])
+    halo_start(grads[4])
 
     arrived(round_qi)
     scale_q = rinv[:, 0:HD]
-    coef = as_columns(total(tp2[0], tp2, 8), 0, 1) * scale_q * scale_q * (1.0 / FEATURES)
+    rowq = rrow[0:1, :]
+    coef = as_columns(total(tp2[0], tp2, 8) * (rowq * rowq * (1.0 / FEATURES)), 0, 1)
+    gden = as_columns(srow[...], 0, HEADS_DEV) * (-1.0 / HD)
     for i in range(HEADS_DEV):
         raw = q[:, head(i)].astype(F32)
         mat = kvb[head(i), :]
-        grad = nt(gn[:, head(i)], mat) + nt(gnl[:, head(i)], mat) + gden[:, head(i)] * zt[pl.ds(i, 1), :]
+        grad = nt(gn[:, head(i)], mat) + nt(gnl[:, head(i)], mat) + gden[:, i * HD : (i + 1) * HD] * zt[pl.ds(i, 1), :]
         gq_o[:, head(i)] = (jnp.where(raw > 0, grad, 0.0) * scale_q - coef * raw).astype(BF16)
-
     stores[2].start()
-
+    backward(0)
+
+    backward(1)
+    arrived(round_gk3)
+    inner = None
+    for i in range(HEADS_DEV):
+        grad = nt(v[:, head(i)], gkb[head(i), :])
+        gfk[:, head(i)] = grad
+        prod = fk[:, head(i)].astype(F32) * grad
+        inner = prod if inner is None else inner + prod
+    inner = row_sums(inner)
     arrived(round_gz2)
     gzt[...] = total(gz2[0], gz2, NZ)
-    arrived(round_gk3)
-    inner = None
-    for i in range(HEADS_DEV):
+    for i in range(HEADS_DEV):
+        high, low = split(jnp.broadcast_to(gzt[pl.ds(i, 1), :], (8, HD)))
         feat = fk[:, head(i)]
-        mat = gkb[head(i), :]
-        grad = nt(v[:, head(i)], mat) + gzt[pl.ds(i, 1), :]
-        gfk[:, head(i)] = grad
-        prod = feat.astype(F32) * grad
-        inner = prod if inner is None else inner + prod
-    tp3[0] = row_sums(inner)
+        inner = inner + nt(high, feat) + nt(low, feat)
+    tp3[0] = inner
     round_ki = tp_round(2, tp3)
     start(round_ki)
+    scale_k = rinv[:, HD : 2 * HD]
     for i in range(HEADS_DEV):
         gv_o[:, head(i)] = nn(fk[:, head(i)], gkb[head(i), :]).astype(BF16)
-
+        grad = gfk[:, head(i)] + gzt[pl.ds(i, 1), :]
+        gfk[:, head(i)] = jnp.where(k[:, head(i)].astype(F32) > 0, grad, 0.0) * scale_k
     stores[4].start()
-
+    backward(2)
     backward(3)
     backward(4)
     stores[5].start()
 
+
     arrived(round_ki)
-    scale_k = rinv[:, HD : 2 * HD]
-    coef = as_columns(total(tp3[0], tp3, 8), 0, 1) * scale_k * scale_k * (1.0 / FEATURES)
-    for i in range(HEADS_DEV):
-        raw = k[:, head(i)].astype(F32)
-        gk_o[:, head(i)] = (jnp.where(raw > 0, gfk[:, head(i)], 0.0) * scale_k - coef * raw).astype(BF16)
+    rowk = rrow[1:2, :]
+    coef = as_columns(total(tp3[0], tp3, 8) * (rowk * rowk * (1.0 / FEATURES)), 0, 1)
+    for i in range(HEADS_DEV):
+        gk_o[:, head(i)] = (gfk[:, head(i)] - coef * k[:, head(i)].astype(F32)).astype(BF16)
     stores[3].start()
 
     for copy in sent:
@@ -508,7 +525,8 @@
         scratch_shapes=[
             narrow(BF16), narrow(BF16), narrow(BF16), narrow(BF16), wide(), vmem((27, CHAN), F32), padded(), padded(),
             narrow(BF16), wide(), narrow(BF16), narrow(BF16), narrow(BF16), wide(),
-            *[narrow(BF16)] * 5, vmem((TOK, 2 * HD), F32), narrow(F32), narrow(F32), narrow(F32),
+            *[narrow(BF16)] * 5, vmem((COLS, TOK), BF16), vmem((COLS, TOK), BF16),
+            vmem((TOK, 2 * HD), F32), vmem((8, TOK), F32), vmem((8, TOK), F32), narrow(F32), narrow(F32),
             vmem((8, 8, TOK), F32), vmem((8, 8, TOK), F32), vmem((8, 8, TOK), F32),
             *state(), *state(),
             vmem((PLANE, 8, HD), F32), vmem((NZ, 8, HD), F32), vmem((8, HD), F32),

time: 65.8 us -> 57.2 us (0.87)
  Pallas kernels: 65 us -> 56.4 us
    pallas_call x1, Pallas kernels: 62.5 us -> 53.8 us  [body(): pl.pallas_call(kernel, out_shape=(att, conv, att, att, att, conv), in_spe...]
where the time goes in v2:
time: 57.2 us; the launch traced here: 57 us
  Pallas kernels  56.4 us (99%)
  between operations  0.64 us (1%)
    pallas_call x1, Pallas kernels, body(): pl.pallas_call(kernel, out_shape=(att, conv, att, att, att, conv), in_spe...  53.8 us
    pallas_call x1, Pallas kernels, body(): pl.pallas_call(store_all, out_shape=(att, conv, att, att, att, conv), in_...  2.55 us

profile of v2, /device:TPU:1, one launch (start us, length us, event | category | flops | bytes accessed | tf_op | source)
XLA Modules:
  0.0 57.0 jit_solution(9939762175926051765)
XLA Ops:
  0.6 53.8 %token_mixing.1 = (bf16[256,384]{1,0:T(8,128)(2,1)}, bf16[256,1280]{1,0:T(8,128)(2,1)}, bf16[256,384]{1,0:T(8,128)(2,1)}, bf16[256,384]{1,0:T(8,128)(2,1)}, bf16...) custom-call(bf16[256,384]{1,0:T(8,128)(2,1)} %q_in.1, bf16[256,384]{1,0:T(8,128)(2,1)} %k_in.1, bf16[256,384]{1,0:T(8,128)(2,1)} %v_in.1, ...), custom_call_target="tpu_custom_call" | custom-call | tf_op jit(solution)/shard_map/token_mixing/pallas_call | solution.py:520
  54.5 2.5 %store_results.1 = (bf16[256,384]{1,0:T(8,128)(2,1)}, bf16[256,1280]{1,0:T(8,128)(2,1)}, bf16[256,384]{1,0:T(8,128)(2,1)}, bf16[256,384]{1,0:T(8,128)(2,1)}, bf1...) custom-call(bf16[256,384]{1,0:T(8,128)(2,1)} %get-tuple-element.12.refs_0_, ...), custom_call_target="tpu_custom_call" | custom-call | tf_op jit(solution)/shard_map/store_results/pallas_call | solution.py:543

commit v3 on v2

--- a/solution.py
+++ b/solution.py
@@ -29,9 +29,10 @@
 NYH, NCORE = 4, 2
 PLANE = NX * NYL
 CHUNK = COLS // PLANE
-HALO_COLS = 256
+HALO_COLS = 128
 HALO_PARTS = CHAN // HALO_COLS
 SEQ = NX * NZ * NYL
+SENT_EARLY = 8
 VMEM_LIMIT = 58 * 1024 * 1024
 
 
@@ -118,41 +119,45 @@
         yl_, x_ = plane_at(j)
         return pl.ds(pl.multiple_of((yl_ * NX + x_) * CHUNK, 16), CHUNK)
 
-    def tp_round(i, buf):
-        return [remote(buf.at[0], buf.at[j], tp_send.at[i, j], tp_recv.at[i, j], tp_dev(j)) for j in tp_order]
-
-    def ring_round(i, src, dst):
-        return [remote(src, dst.at[j], ring_send.at[i, j], ring_recv.at[i, j], ring_dev(j)) for j in ring_order]
-
-    def plane_round(i, src, dst):
-        return [remote(src, dst.at[j], plane_send.at[i, j], plane_recv.at[i, j], plane_dev(j)) for j in plane_order]
-
-    def plane_scatter(i, src, dst):
-        return [
-            remote(src.at[plane_rows(j)], dst.at[j], plane_send.at[i, j], plane_recv.at[i, j], plane_dev(j))
-            for j in plane_order
-        ]
-
-    def plane_gather(i, buf):
-        return [
-            remote(buf.at[mine], buf.at[mine], plane_send.at[i, j], plane_recv.at[i, j], plane_dev(j))
-            for j in plane_order
-        ]
+    def exchange(copies, whole, send, recv):
+        return copies, pltpu.make_async_copy(whole, whole, send), pltpu.make_async_copy(whole, whole, recv)
 
     tp_order = (4, 5, 2, 3, 6, 7, 1)
     ring_order = (4, 3, 5, 2, 6, 1, 7)
     plane_order = (6, 2, 5, 7, 1, 3, 4)
+    others = pl.ds(1, 7)
+
+    def tp_round(i, buf):
+        sems = tp_send.at[i], tp_recv.at[i]
+        return exchange([remote(buf.at[0], buf.at[j], *sems, tp_dev(j)) for j in tp_order], buf.at[others], *sems)
+
+    def ring_round(i, src, dst):
+        sems = ring_send.at[i], ring_recv.at[i]
+        return exchange([remote(src, dst.at[j], *sems, ring_dev(j)) for j in ring_order], dst.at[others], *sems)
+
+    def plane_round(i, src, dst):
+        sems = plane_send.at[i], plane_recv.at[i]
+        return exchange([remote(src, dst.at[j], *sems, plane_dev(j)) for j in plane_order], dst.at[others], *sems)
+
+    def plane_scatter(i, src, dst):
+        sems = plane_send.at[i], plane_recv.at[i]
+        copies = [remote(src.at[plane_rows(j)], dst.at[j], *sems, plane_dev(j)) for j in plane_order]
+        return exchange(copies, dst.at[others], *sems)
+
+    def plane_gather(i, buf):
+        sems = plane_send.at[i], plane_recv.at[i]
+        copies = [remote(buf.at[mine], buf.at[mine], *sems, plane_dev(j)) for j in plane_order]
+        return exchange(copies, buf.at[pl.ds(0, (PLANE - 1) * CHUNK)], *sems)
 
     sent = []
 
-    def start(copies):
-        for copy in copies:
+    def start(round_):
+        for copy in round_[0]:
             copy.start()
-        sent.extend(copies)
-
-    def arrived(copies):
-        for copy in copies:
-            copy.wait_recv()
+        sent.append(round_[1])
+
+    def arrived(round_):
+        round_[2].wait()
 
     def total(own, buf, count):
         for j in range(1, count):
@@ -166,10 +171,10 @@
     def halo_copies(i, part, buf, src_up, src_down):
         cols = pl.ds(part * HALO_COLS, HALO_COLS)
         to_next = remote(
-            src_up(cols), buf.at[0, body_rows, cols], halo_send.at[i, 0, part], halo_recv.at[i, 0, part], up
+            src_up(cols), buf.at[0, body_rows, cols], halo_send.at[i, 0], halo_recv.at[i, 0, part], up
         )
         to_prev = remote(
-            src_down(cols), buf.at[3, body_rows, cols], halo_send.at[i, 1, part], halo_recv.at[i, 1, part], down
+            src_down(cols), buf.at[3, body_rows, cols], halo_send.at[i, 1], halo_recv.at[i, 1, part], down
         )
         return to_next, to_prev
 
@@ -199,14 +204,16 @@
         def _():
             copies[1].wait_recv()
 
-    def halo_sent(copies):
+    def halo_sent(i, buf):
+        frame = buf.at[0, body_rows]
+
         @pl.when(s < SEQ - 1)
         def _():
-            copies[0].wait_send()
+            pltpu.make_async_copy(frame, frame, halo_send.at[i, 0]).wait()
 
         @pl.when(s > 0)
         def _():
-            copies[1].wait_send()
+            pltpu.make_async_copy(frame, frame, halo_send.at[i, 1]).wait()
 
     loads = [
         pltpu.make_async_copy(src, dst, in_sem.at[i])
@@ -251,6 +258,8 @@
     start(round_sq)
     halo_start(hidden[0])
     halo_start(hidden[1])
+    halo_start(hidden[2])
+    halo_start(hidden[3])
 
     blank = jnp.zeros((4, WID, CHAN), BF16)
     for buf in (hp, gp):
@@ -328,8 +337,8 @@
     rrow[...] = lax.rsqrt(total(tp1[0], tp1, 8) * (1.0 / FEATURES) + EPS)
     scale_k = rrow[1:2, :]
     for i in range(HEADS_DEV):
-        feat, low = split(kt[head(i), :].astype(F32) * scale_k)
-        z1[0, pl.ds(i, 1), :] = (nt(ones, feat) + nt(ones, low))[0:1] * (1.0 / TOKENS)
+        feat = (kt[head(i), :].astype(F32) * scale_k).astype(BF16)
+        z1[0, pl.ds(i, 1), :] = nt(ones, feat)[0:1] * (1.0 / TOKENS)
         part = nn(feat, v[:, head(i)]) * (1.0 / TOKENS)
         kvp[head(i), :] = part
         kvs[head(i), :] = part.astype(BF16)
@@ -337,7 +346,6 @@
     start(round_z1)
     round_kv1 = plane_scatter(0, kvs, kv1)
     start(round_kv1)
-    halo_start(hidden[2])
 
     rinv[...] = as_columns(rrow[...], 0, 2)
     scale_q = rinv[:, 0:HD]
@@ -347,8 +355,11 @@
         fk[:, head(i)] = (jnp.maximum(k[:, head(i)].astype(F32), 0.0) * scale_k).astype(BF16)
         qt[head(i), :] = (qt[head(i), :].astype(F32) * rrow[0:1, :]).astype(BF16)
 
+    halo_start(hidden[4])
     forward(0)
     forward(1)
+    forward(2)
+    halo_start(hidden[5])
     arrived(round_z1)
     z2[0] = total(z1[0], z1, PLANE)
     round_z2 = ring_round(0, z2.at[0], z2)
@@ -358,10 +369,12 @@
     kv2[0] = kvc[...].astype(BF16)
     round_kv2 = ring_round(1, kv2.at[0], kv2)
     start(round_kv2)
-    halo_start(hidden[3])
-
-
-    forward(2)
+    halo_start(hidden[6])
+
+
+    forward(3)
+    forward(4)
+    halo_start(hidden[7])
     arrived(round_z2)
     zt[...] = total(z2[0], z2, NZ)
     for i in range(HEADS_DEV):
@@ -381,16 +394,16 @@
     kvb[mine, :] = total(kvc[...], kv2, NZ).astype(BF16)
     round_kv3 = plane_gather(2, kvb)
     start(round_kv3)
-    halo_start(hidden[4])
-    forward(3)
+    halo_start(hidden[8])
+    forward(5)
+    halo_start(hidden[9])
+    forward(6)
 
     arrived(round_gk1)
     gkc[...] = total(gkp[mine, :], gk1, PLANE)
     gk2[0] = gkc[...].astype(BF16)
     round_gk2 = ring_round(2, gk2.at[0], gk2)
     start(round_gk2)
-    halo_start(grads[0])
-    halo_start(grads[1])
 
     arrived(round_kv3)
     for i in range(HEADS_DEV):
@@ -409,8 +422,11 @@
     round_qi = tp_round(1, tp2)
     start(round_qi)
     stores[0].start()
-    forward(4)
-    stores[1].start()
+    halo_start(grads[0])
+    halo_start(grads[1])
+    forward(7)
+    forward(8)
+    halo_start(grads[2])
 
 
     arrived(round_gk2)
@@ -421,9 +437,10 @@
     gz2[0] = total(gz1[0], gz1, PLANE)
     round_gz2 = ring_round(3, gz2.at[0], gz2)
     start(round_gz2)
-    halo_start(grads[2])
     halo_start(grads[3])
     halo_start(grads[4])
+    forward(9)
+    stores[1].start()
 
     arrived(round_qi)
     scale_q = rinv[:, 0:HD]
@@ -437,8 +454,15 @@
         gq_o[:, head(i)] = (jnp.where(raw > 0, grad, 0.0) * scale_q - coef * raw).astype(BF16)
     stores[2].start()
     backward(0)
-
+    halo_start(grads[5])
     backward(1)
+    halo_start(grads[6])
+    backward(2)
+
+    for copy in sent[:SENT_EARLY]:
+        copy.wait()
+    halo_sent(0, hp)
+
     arrived(round_gk3)
     inner = None
     for i in range(HEADS_DEV):
@@ -456,15 +480,22 @@
     tp3[0] = inner
     round_ki = tp_round(2, tp3)
     start(round_ki)
+    halo_start(grads[7])
+    halo_start(grads[8])
+    halo_start(grads[9])
     scale_k = rinv[:, HD : 2 * HD]
     for i in range(HEADS_DEV):
         gv_o[:, head(i)] = nn(fk[:, head(i)], gkb[head(i), :]).astype(BF16)
         grad = gfk[:, head(i)] + gzt[pl.ds(i, 1), :]
         gfk[:, head(i)] = jnp.where(k[:, head(i)].astype(F32) > 0, grad, 0.0) * scale_k
     stores[4].start()
-    backward(2)
     backward(3)
     backward(4)
+    backward(5)
+    backward(6)
+    backward(7)
+    backward(8)
+    backward(9)
     stores[5].start()
 
 
@@ -475,10 +506,9 @@
         gk_o[:, head(i)] = (gfk[:, head(i)] - coef * k[:, head(i)].astype(F32)).astype(BF16)
     stores[3].start()
 
-    for copy in sent:
-        copy.wait_send()
-    for copies in hidden + grads:
-        halo_sent(copies)
+    for copy in sent[SENT_EARLY:]:
+        copy.wait()
+    halo_sent(1, gp)
     for copy in stores:
         copy.wait()
 
@@ -532,8 +562,8 @@
             vmem((PLANE, 8, HD), F32), vmem((NZ, 8, HD), F32), vmem((8, HD), F32),
             vmem((PLANE, 8, HD), F32), vmem((NZ, 8, HD), F32), vmem((8, HD), F32),
             dma((8,)), dma((6,)),
-            dma((3, 8)), dma((3, 8)), dma((6, PLANE)), dma((6, PLANE)), dma((4, NZ)), dma((4, NZ)),
-            dma((2, 2, HALO_PARTS)), dma((2, 2, HALO_PARTS)),
+            dma((3,)), dma((3,)), dma((6,)), dma((6,)), dma((4,)), dma((4,)),
+            dma((2, 2)), dma((2, 2, HALO_PARTS)),
         ],
         compiler_params=pltpu.CompilerParams(
             collective_id=0, has_side_effects=True, vmem_limit_bytes=VMEM_LIMIT

time: 57.2 us -> 54.9 us (0.960)
  Pallas kernels: 56.4 us -> 54.1 us
    pallas_call x1, Pallas kernels: 53.8 us -> 51.5 us  [body(): pl.pallas_call(kernel, out_shape=(att, conv, att, att, att, conv), in_spe...]
where the time goes in v3:
time: 54.9 us; the launch traced here: 54.7 us
  Pallas kernels  54.1 us (99%)
  between operations  0.64 us (1%)
    pallas_call x1, Pallas kernels, body(): pl.pallas_call(kernel, out_shape=(att, conv, att, att, att, conv), in_spe...  51.5 us
    pallas_call x1, Pallas kernels, body(): pl.pallas_call(store_all, out_shape=(att, conv, att, att, att, conv), in_...  2.55 us

profile of v3, /device:TPU:1, one launch (start us, length us, event | category | flops | bytes accessed | tf_op | source)
XLA Modules:
  0.0 54.7 jit_solution(16960972036021046875)
XLA Ops:
  0.6 51.5 %token_mixing.1 = (bf16[256,384]{1,0:T(8,128)(2,1)}, bf16[256,1280]{1,0:T(8,128)(2,1)}, bf16[256,384]{1,0:T(8,128)(2,1)}, bf16[256,384]{1,0:T(8,128)(2,1)}, bf16...) custom-call(bf16[256,384]{1,0:T(8,128)(2,1)} %q_in.1, bf16[256,384]{1,0:T(8,128)(2,1)} %k_in.1, bf16[256,384]{1,0:T(8,128)(2,1)} %v_in.1, ...), custom_call_target="tpu_custom_call" | custom-call | tf_op jit(solution)/shard_map/token_mixing/pallas_call | solution.py:550
  52.2 2.5 %store_results.1 = (bf16[256,384]{1,0:T(8,128)(2,1)}, bf16[256,1280]{1,0:T(8,128)(2,1)}, bf16[256,384]{1,0:T(8,128)(2,1)}, bf16[256,384]{1,0:T(8,128)(2,1)}, bf1...) custom-call(bf16[256,384]{1,0:T(8,128)(2,1)} %get-tuple-element.12.refs_0_, ...), custom_call_target="tpu_custom_call" | custom-call | tf_op jit(solution)/shard_map/store_results/pallas_call | solution.py:573

commit v4 on v3

--- a/solution.py
+++ b/solution.py
@@ -413,9 +413,7 @@
         att_o[:, head(i)] = att.astype(BF16)
         inner = row_sums(g[:, head(i)].astype(F32) * inv * att)
         srow[pl.ds(i, 1), :] = inner[0:1]
-        high, low = split(inner)
-        feat = fq[:, head(i)]
-        gz1[0, pl.ds(i, 1), :] = (nn(high, feat) + nn(low, feat))[0:1] * (-1.0 / HD / TOKENS)
+        gz1[0, pl.ds(i, 1), :] = nn(inner.astype(BF16), fq[:, head(i)])[0:1] * (-1.0 / HD / TOKENS)
     round_gz1 = plane_round(4, gz1.at[0], gz1)
     start(round_gz1)
     tp2[0] = jnp.broadcast_to(srow[0:1, :] + srow[1:2, :] + srow[2:3, :], (8, TOK))

time: 54.9 us -> 54.7 us (level)
  no operation moved by 1% of the time
where the time goes in v4:
time: 54.7 us; the launch traced here: 54.5 us
  Pallas kernels  53.9 us (99%)
  between operations  0.64 us (1%)
    pallas_call x1, Pallas kernels, body(): pl.pallas_call(kernel, out_shape=(att, conv, att, att, att, conv), in_spe...  51.3 us
    pallas_call x1, Pallas kernels, body(): pl.pallas_call(store_all, out_shape=(att, conv, att, att, att, conv), in_...  2.55 us

profile of v4, /device:TPU:1, one launch (start us, length us, event | category | flops | bytes accessed | tf_op | source)
XLA Modules:
  0.0 54.5 jit_solution(18110573809683652545)
XLA Ops:
  0.6 51.3 %token_mixing.1 = (bf16[256,384]{1,0:T(8,128)(2,1)}, bf16[256,1280]{1,0:T(8,128)(2,1)}, bf16[256,384]{1,0:T(8,128)(2,1)}, bf16[256,384]{1,0:T(8,128)(2,1)}, bf16...) custom-call(bf16[256,384]{1,0:T(8,128)(2,1)} %q_in.1, bf16[256,384]{1,0:T(8,128)(2,1)} %k_in.1, bf16[256,384]{1,0:T(8,128)(2,1)} %v_in.1, ...), custom_call_target="tpu_custom_call" | custom-call | tf_op jit(solution)/shard_map/token_mixing/pallas_call | solution.py:548
  52.0 2.5 %store_results.1 = (bf16[256,384]{1,0:T(8,128)(2,1)}, bf16[256,1280]{1,0:T(8,128)(2,1)}, bf16[256,384]{1,0:T(8,128)(2,1)}, bf16[256,384]{1,0:T(8,128)(2,1)}, bf1...) custom-call(bf16[256,384]{1,0:T(8,128)(2,1)} %get-tuple-element.12.refs_0_, ...), custom_call_target="tpu_custom_call" | custom-call | tf_op jit(solution)/shard_map/store_results/pallas_call | solution.py:571
